TPU v7x, 512 devices: a whole 4x4x16 slice. The times are simulated.
512 devices in a mesh: wn: 16 (over z_lo, core), sw: 32 (over z_hi, y, x).
Axes of the slice: x: 4, y: 4, z: 16 (z_hi: 2, z_lo: 8; z = z_hi * 8 + z_lo), core: 2. Of those that a mesh axis runs over, the one named last changes fastest.
Arguments:
- salinity: bfloat16 [6, 6144, 3072], P(None, ('wn', 'sw')), may hold values from -6 to 6
- velocity: bfloat16 [3, 2, 16, 128, 1024], P(None, None, None, 'sw', 'wn'), may hold values from -6 to 6
- wall_index: int32 [3072], replicated, may hold values from 0 to 1022, as said below
- wall_weight: float32 [3072], replicated, may hold values from 0 to 1
- spacing: float32 [3072], replicated, may hold values from 0.5 to 2
Outputs:
- salinity_new: bfloat16 [6, 6144, 3072], P(None, ('wn', 'sw'))
- coarse_salinity: bfloat16 [2, 16, 128, 1024], P(None, None, 'sw', 'wn')
Inputs may be any that keep to these rules, and one draw needn't show every extreme that they name: `wall_index`: nondecreasing; the value 1024 - 2 occurs exactly 6 times, every other value between 1 and 5 times.
All inputs are finite; a program needn't handle non-finite values.
Results may differ from a plain program's by a relative error of at most 0.0039.
Values may be sent and summed in bfloat16 or wider, within the bound.
No kernel may reach another device: no remote copies, remote signals or barrier semaphores. Data moves between devices by JAX's collectives and lax.ppermute only.
A program may use at most 64 MiB of HBM per device.

v0:
```python
import jax
import jax.numpy as jnp
from jax import lax
from jax.sharding import PartitionSpec as P

time_step = 0.5
runge_gamma = 8.0 / 15.0
diffusivity = 0.3


def padded(cells, sides, width):
    for axis, dim in sides:
        count = lax.axis_size(axis)
        head = lax.slice_in_dim(cells, 0, width, axis=dim)
        tail = lax.slice_in_dim(cells, cells.shape[dim] - width, cells.shape[dim], axis=dim)
        cells = jnp.concatenate(
            [
                lax.ppermute(tail, axis, [(i, (i + 1) % count) for i in range(count)]),
                cells,
                lax.ppermute(head, axis, [((i + 1) % count, i) for i in range(count)]),
            ],
            axis=dim,
        )
    return cells


def block_layout(coarse_count):
    window = min(coarse_count, 256)
    fine_width = 3 * min(coarse_count, 128)
    block_count = 3 * coarse_count // fine_width
    starts = [
        min(max(b * fine_width // 3 - 64, 0), coarse_count - window) for b in range(block_count)
    ]
    return (window, fine_width, starts)


def weight_block(wall_index, wall_weight, start, window, fine_start, fine_width):
    index_part = wall_index[fine_start : fine_start + fine_width]
    weight_part = wall_weight[fine_start : fine_start + fine_width]
    rows = start + jnp.arange(window, dtype=jnp.int32)
    lower_hit = (rows[:, None] == index_part[None, :]).astype(jnp.float32)
    upper_hit = (rows[:, None] == (index_part + 1)[None, :]).astype(jnp.float32)
    return lower_hit * (1.0 - weight_part)[None, :] + upper_hit * weight_part[None, :]


def wall_interpolate(values, wall_index, wall_weight):
    window, fine_width, starts = block_layout(values.shape[-1])
    pieces = []
    for number, start in enumerate(starts):
        matrix = weight_block(
            wall_index, wall_weight, start, window, number * fine_width, fine_width
        )
        pieces.append(
            jnp.einsum(
                "cpyk,kj->cpyj",
                values[..., start : start + window],
                matrix,
                precision=lax.Precision.HIGHEST,
            )
        )
    return jnp.concatenate(pieces, axis=-1)


def wall_restrict(grouped, wall_index, wall_weight, coarse_count):
    window, fine_width, starts = block_layout(coarse_count)
    total = jnp.zeros(grouped.shape[:-1] + (coarse_count,), jnp.float32)
    for number, start in enumerate(starts):
        matrix = weight_block(
            wall_index, wall_weight, start, window, number * fine_width, fine_width
        )
        part = grouped[..., number * fine_width : (number + 1) * fine_width]
        total = total.at[..., start : start + window].add(
            jnp.einsum("pyj,kj->pyk", part, matrix, precision=lax.Precision.HIGHEST)
        )
    return total


def fine_velocity(coarse_block, wall_index, wall_weight):
    values = coarse_block.astype(jnp.float32)
    normal = wall_interpolate(values, wall_index, wall_weight)
    center = normal[:, :, 1:-1]
    previous = normal[:, :, :-2]
    following = normal[:, :, 2:]
    one_third = 1.0 / 3.0
    streamwise = jnp.stack(
        [
            one_third * previous + 2.0 * one_third * center,
            center,
            2.0 * one_third * center + one_third * following,
        ],
        axis=3,
    )
    block_shape = streamwise.shape
    streamwise = streamwise.reshape(
        block_shape[0], block_shape[1], block_shape[2] * 3, block_shape[4]
    )
    plane_below = jnp.roll(streamwise, 1, axis=1)
    plane_above = jnp.roll(streamwise, -1, axis=1)
    across = jnp.stack(
        [
            one_third * plane_below + 2.0 * one_third * streamwise,
            streamwise,
            2.0 * one_third * streamwise + one_third * plane_above,
        ],
        axis=2,
    )
    return across.reshape(block_shape[0], block_shape[1] * 3, block_shape[2] * 3, block_shape[4])


def advance(salinity_block, velocity_fine, spacing):
    field = salinity_block.astype(jnp.float32)
    middle = field[:, 1:-1]
    forward = field[:, 2:]
    behind = field[:, :-2]
    wall_low = jnp.concatenate([-middle[:, :, :1], middle[:, :, :-1]], axis=2)
    wall_high = jnp.concatenate([middle[:, :, 1:], -middle[:, :, -1:]], axis=2)
    span_low = jnp.roll(middle, 1, axis=0)
    span_high = jnp.roll(middle, -1, axis=0)
    centers = 0.5 * (spacing[:-1] + spacing[1:])
    gap_low = jnp.concatenate([spacing[:1], centers])
    gap_high = jnp.concatenate([centers, spacing[-1:]])
    slope = (wall_high - wall_low) / (gap_low + gap_high)
    curvature = ((wall_high - middle) / gap_high - (middle - wall_low) / gap_low) / spacing
    laplace = curvature + (forward - 2.0 * middle + behind) + (span_high - 2.0 * middle + span_low)
    transport = (
        velocity_fine[0] * 0.5 * (forward - behind)
        + velocity_fine[1] * slope
        + velocity_fine[2] * 0.5 * (span_high - span_low)
    )
    return (middle + time_step * runge_gamma * (diffusivity * laplace - transport)).astype(
        jnp.bfloat16
    )


def restrict(updated, wall_index, wall_weight):
    values = updated.astype(jnp.float32)
    plane_count, row_count, cell_count = updated.shape
    grouped = (
        values.reshape(plane_count // 3, 3, row_count // 3, 3, cell_count).sum(axis=(1, 3)) / 3.0
    )
    total = wall_restrict(grouped, wall_index, wall_weight, cell_count // 3)
    return (total / 3.0).astype(jnp.bfloat16)


def body(salinity, velocity, wall_index, wall_weight, spacing):
    arrived = lax.all_to_all(velocity, "wn", split_axis=2, concat_axis=4, tiled=True)[:, :, 0]
    coarse_block = padded(arrived, ((("wn", "sw"), 2),), 1)
    padded_salinity = padded(salinity, ((("wn", "sw"), 1),), 1)
    velocity_fine = fine_velocity(coarse_block, wall_index, wall_weight)
    updated = advance(padded_salinity, velocity_fine, spacing)
    restricted = restrict(updated, wall_index, wall_weight)
    returned = lax.all_to_all(restricted[:, None], "wn", split_axis=3, concat_axis=1, tiled=True)
    return (updated, returned)


def solution(mesh):
    in_specs = (P(None, ("wn", "sw"), None), P(None, None, None, "sw", "wn"), P(), P(), P())
    out_specs = (P(None, ("wn", "sw"), None), P(None, None, "sw", "wn"))
    return jax.shard_map(body, mesh=mesh, in_specs=in_specs, out_specs=out_specs, check_vma=False)
```

profile of v0, /device:TPU:30, one launch (start us, length us, event | category | flops | bytes accessed | tf_op | source)
XLA Modules:
  0.0 133.4 jit_solution(10050217018768030281)
XLA Ops:
  0.6 1.0 copy.45
  1.6 0.7 reshape.411
  2.4 12.7 %all-to-all-start = ((bf16[16,2,768]{2,1,0:T(2,128)(2,1)}), bf16[16,2,768]{2,1,0:T(2,128)(2,1)}, u32[]{:S(2)}, u32[]{:S(2)}) async-start(bf16[16,2,768]{2,1,0:T(2,128)(2,1)} %reshape.411), calls=%async_computation | async-start | bytes 98304 | tf_op jit(solution)/shard_map/all_to_all | solution.py:146
  15.1 1.2 fusion.188
  16.2 7.8 %collective-permute-start = (bf16[6,1,3072]{2,1,0:T(2,128)(2,1)S(1)}, bf16[6,1,3072]{2,1,0:T(2,128)(2,1)S(1)}, u32[]{:S(2)}, u32[]{:S(2)}) collective-permute-start(bf16[6,1,3072]{2,1,0:T(2,128)(2,1)S(1)} %get-tuple-element.114), channel_id=1, source_target_pairs={{0,1},{1,2},{2,3},{3,4},{4,5},{5,6},{6,7},{7,8},{8,9},{9,10},{10,1... | collective-permute-start | bytes 110600 | tf_op jit(solution)/shard_map/ppermute | solution.py:18
  24.0 1.9 %collective-permute-start.1 = (bf16[6,1,3072]{2,1,0:T(2,128)(2,1)S(1)}, bf16[6,1,3072]{2,1,0:T(2,128)(2,1)S(1)}, u32[]{:S(2)}, u32[]{:S(2)}) collective-permute-start(bf16[6,1,3072]{2,1,0:T(2,128)(2,1)S(1)} %get-tuple-element.115), channel_id=1, source_target_pairs={{1,0},{2,1},{3,2},{4,3},{5,4},{6,5},{7,6},{8,7},{9,8},{10,9},{11,1... | collective-permute-start | bytes 110600 | tf_op jit(solution)/shard_map/ppermute | solution.py:20
  26.0 0.6 iota_add_fusion.6
  26.6 0.6 iota_add_fusion.5
  27.1 0.6 iota_add_fusion.4
  27.7 0.6 iota_add_fusion.3
  28.3 0.6 iota_add_fusion.2
  28.9 0.6 iota_add_fusion.1
  29.5 1.4 %fusion.190 = (f32[1]{0:T(128)}, f32[1]{0:T(128)}) fusion(f32[3072]{0:T(1024)} %param.25), kind=kLoop, calls=%fused_computation.266 | loop fusion | bytes 16 | tf_op jit(solution)/shard_map/slice | solution.py:120
  30.8 0.9 add_multiply_fusion
  31.7 1.5 %fusion.191 = (s32[384]{0:T(512)S(1)}, s32[384]{0:T(512)}, s32[384]{0:T(512)}, s32[384]{0:T(512)}, s32[384]{0:T(512)}, /*index=5*/s32[384]{0:T(512)}, s32[384]{0...) fusion(s32[3072]{0:T(1024)} %param.23), kind=kLoop, calls=%fused_computation.267 | loop fusion | flops 3072 | bytes 36864 | tf_op jit(solution)/shard_map/slice | solution.py:38
  33.2 1.5 %broadcast_subtract_fusion = (f32[384]{0:T(512)}, f32[384]{0:T(512)}, f32[384]{0:T(512)}, f32[384]{0:T(512)}, f32[384]{0:T(512)}, /*index=5*/f32[384]{0:T(512)},...) fusion(f32[3072]{0:T(1024)} %param.24), kind=kLoop, calls=%fused_computation.236 | loop fusion | flops 3072 | bytes 36864 | tf_op jit(solution)/shard_map/sub | solution.py:43
  34.7 2.0 %fusion.184 = (f32[3072]{0:T(1024)S(1)}, f32[3072]{0:T(1024)}, f32[3072]{0:T(1024)}) fusion(f32[1]{0:T(128)} %get-tuple-element.122, f32[3071]{0:T(1024)S(1)} %add_multiply_fusion, f32[1]{0:T(128)} %get-tuple-element.121), kind=kLoop, calls=%fused_computation.260 | loop fusion | flops 9216 | bytes 49156 | tf_op jit(solution)/shard_map/add | solution.py:122
  36.7 0.6 iota_add_fusion
  37.3 6.1 %collective-permute-done.1 = bf16[6,1,3072]{2,1,0:T(2,128)(2,1)S(1)} collective-permute-done((bf16[6,1,3072]{2,1,0:T(2,128)(2,1)S(1)}, bf16[6,1,3072]{2,1,0:T(2,128)(2,1)S(1)}, u32[]{:S(2)}, u32[]{:S(2)}) %collective-permute-start.1) | collective-permute-done | bytes 36896 | tf_op jit(solution)/shard_map/ppermute | solution.py:20
  43.4 0.6 copy-done.6
  44.4 1.5 %fusion.186 = (f32[5,12,3072]{2,1,0:T(8,128)}, f32[5,12,3072]{2,1,0:T(8,128)}) fusion(f32[6,14,3072]{2,1,0:T(8,128)S(1)} %maximum_convert_fusion), kind=kLoop, calls=%fused_computation.262 | loop fusion | bytes 2949120 | tf_op jit(solution)/shard_map/jit(_roll_static)/slice | solution.py:118
  45.8 0.4 fusion.185
  46.3 0.8 fusion.187
  47.0 1.6 %reshape.412 = bf16[16,3,2,4,64]{4,3,2,1,0:T(4,128)(2,1)} reshape(bf16[16,2,768]{2,1,0:T(2,128)(2,1)} %all-to-all-done) | data formatting | bytes 98304
  48.6 0.9 bitcast_bitcast_fusion
  49.5 0.6 copy.26
  50.2 1.6 %squeeze.8 = bf16[3,2,4,1024]{3,2,1,0:T(4,128)(2,1)} reshape(bf16[3,2,1,4,16,64]{5,4,3,1,0,2:T(8,128)(2,1)} %copy.26) | data formatting | bytes 98304 | tf_op jit(solution)/shard_map/squeeze | solution.py:146
  51.8 0.9 fusion.189
  52.7 11.4 %collective-permute-start.2 = (bf16[3,2,1,1024]{3,2,1,0:T(2,128)(2,1)S(1)}, bf16[3,2,1,1024]{3,2,1,0:T(2,128)(2,1)S(1)}, u32[]{:S(2)}, u32[]{:S(2)}) collective-permute-start(bf16[3,2,1,1024]{3,2,1,0:T(2,128)(2,1)S(1)} %get-tuple-element.119), channel_id=1, source_target_pairs={{0,1},{1,2},{2,3},{3,4},{4,5},{5,6},{6,7},{7,8},{8,9},{9,10},{10,1... | collective-permute-start | bytes 36872 | tf_op jit(solution)/shard_map/ppermute | solution.py:18
  64.1 1.9 %collective-permute-start.3 = (bf16[3,2,1,1024]{3,2,1,0:T(2,128)(2,1)S(1)}, bf16[3,2,1,1024]{3,2,1,0:T(2,128)(2,1)S(1)}, u32[]{:S(2)}, u32[]{:S(2)}) collective-permute-start(bf16[3,2,1,1024]{3,2,1,0:T(2,128)(2,1)S(1)} %get-tuple-element.120), channel_id=1, source_target_pairs={{1,0},{2,1},{3,2},{4,3},{5,4},{6,5},{7,6},{8,7},{9,8},{10,9},{11,1... | collective-permute-start | bytes 36872 | tf_op jit(solution)/shard_map/ppermute | solution.py:20
  66.1 0.9 convert_negate_fusion.1
  67.0 15.8 %collective-permute-done.3 = bf16[3,2,1,1024]{3,2,1,0:T(2,128)(2,1)S(1)} collective-permute-done((bf16[3,2,1,1024]{3,2,1,0:T(2,128)(2,1)S(1)}, bf16[3,2,1,1024]{3,2,1,0:T(2,128)(2,1)S(1)}, u32[]{:S(2)}, u32[]{:S(2)}) %collective-permute-start.3) | collective-permute-done | bytes 12320 | tf_op jit(solution)/shard_map/ppermute | solution.py:20
  82.8 0.9 pad_maximum_fusion.6
  83.7 1.0 convolution_dynamic-update-slice_fusion.7
  84.8 1.1 convolution_dynamic-update-slice_fusion.6
  86.0 0.4 convolution_dynamic-update-slice_fusion.5
  89.2 0.7 copy.27
  89.9 0.7 slice_bitcast_fusion.1
  90.6 1.4 %fusion.7 = f32[3,2,1,12,3072]{4,1,3,2,0:T(2,128)S(1)} fusion(f32[3,1,1,12,3072]{4,1,3,2,0:T(1,128)S(1)} %get-tuple-element.111, f32[3,1,1,12,3072]{4,1,3,2,0:T(1,128)S(1)} %get-tuple-element.110, f32[3,2,1,12,3072]{4,1,3,2,0:T(2,128)S(1)} %bitcast.125), kind=kLoop, calls=%fused_computation.34 | loop fusion | flops 884736 | bytes 2654208 | tf_op jit(solution)/shard_map/add | solution.py:101
  92.0 1.1 pad_maximum_fusion
  93.0 1.4 %slice_multiply_fusion.1 = (f32[1,2,3,12,3072]{4,1,3,2,0:T(2,128)S(1)}, f32[1,2,3,12,3072]{4,1,3,2,0:T(2,128)S(1)}, f32[1,2,3,12,3072]{4,1,3,2,0:T(2,128)S(1)}) fusion(f32[3,2,3,12,3072]{4,1,3,2,0:T(2,128)S(1)} %pad_maximum_fusion), kind=kLoop, calls=%fused_computation.31 | loop fusion | flops 442368 | bytes 5308416 | tf_op jit(solution)/shard_map/mul | solution.py:126
  95.8 0.5 copy-done
  96.6 2.9 %fusion.4 = bf16[6,12,3072]{2,1,0:T(8,128)(2,1)} fusion(f32[1,2,3,12,3072]{4,3,2,1,0:T(8,128)S(1)} %copy.33, f32[1,2,3,12,3072]{4,3,2,1,0:T(8,128)S(1)} %copy.32, f32[1,2,3,12,3072]{4,3,2,1,0:T(8,128)S(1)} %copy.31, f32[5,12,3072]{2,1,0:T(8,128)S(1)} %copy-done.1, f32[1,12,3072]{2,1,0:T(8,128)S(1)} %copy-done.4, f32[1,12,3072]{2,1,0:T(8,128)S(1)} %copy-done.3, ...), kind=kLoop, calls=%fused_computation.10 | loop fusion | flops 6856704 | bytes 9338880 | tf_op jit(solution)/shard_map/convert_element_type | solution.py:130
  99.6 1.5 %reshape.394 = f32[2,3,4,3,3072]{4,3,2,1,0:T(4,128)S(1)} reshape(bf16[6,12,3072]{2,1,0:T(8,128)(2,1)} %fusion.4) | data formatting | bytes 1327104 | tf_op jit(solution)/shard_map/reshape | solution.py:139
  101.2 0.4 reduce_sum.9
  101.8 0.5 fusion.23
  102.4 0.5 convolution_add_fusion.6
  103.0 0.5 scatter-add.29
  103.6 0.5 convolution_add_fusion.5
  104.2 0.5 scatter-add.30
  104.8 0.5 convolution_add_fusion.4
  105.4 0.5 scatter-add.31
  105.9 0.5 convolution_add_fusion.3
  106.5 0.5 scatter-add.34
  107.1 0.5 convolution_add_fusion.2
  107.6 0.5 scatter-add.35
  108.2 0.5 convolution_add_fusion.1
  108.7 0.5 scatter-add.36
  109.3 0.5 fusion.6
  109.8 0.5 copy.34
  110.3 0.8 reshape.413
  111.1 20.1 %all_to_all.33 = bf16[16,2,256]{2,1,0:T(2,128)(2,1)S(1)} all-to-all(bf16[16,2,256]{2,1,0:T(2,128)(2,1)S(1)} %reshape.413), channel_id=1, replica_groups=mesh['wn'=16,'sw'=32] {'wn'}, dimensions={0} | all-to-all | bytes 32768 | tf_op jit(solution)/shard_map/all_to_all | solution.py:152
  131.2 1.1 reshape.414
  132.4 1.1 copy.35
  (169 shorter events, 4.8 us)
Async XLA Ops:
  0.6 43.4 %copy-start.2 = (bf16[6,12,3072]{2,1,0:T(8,128)(2,1)S(1)}, bf16[6,12,3072]{2,1,0:T(8,128)(2,1)}, u32[]{:S(2)}) copy-start(bf16[6,12,3072]{2,1,0:T(8,128)(2,1)} %param.21) | copy-start | bytes 1327108
  2.4 44.7 %all-to-all-start = ((bf16[16,2,768]{2,1,0:T(2,128)(2,1)}), bf16[16,2,768]{2,1,0:T(2,128)(2,1)}, u32[]{:S(2)}, u32[]{:S(2)}) async-start(bf16[16,2,768]{2,1,0:T(2,128)(2,1)} %reshape.411), calls=%async_computation | async-start | bytes 98304 | tf_op jit(solution)/shard_map/all_to_all | solution.py:146
  16.2 21.1 %collective-permute-start = (bf16[6,1,3072]{2,1,0:T(2,128)(2,1)S(1)}, bf16[6,1,3072]{2,1,0:T(2,128)(2,1)S(1)}, u32[]{:S(2)}, u32[]{:S(2)}) collective-permute-start(bf16[6,1,3072]{2,1,0:T(2,128)(2,1)S(1)} %get-tuple-element.114), channel_id=1, source_target_pairs={{0,1},{1,2},{2,3},{3,4},{4,5},{5,6},{6,7},{7,8},{8,9},{9,10},{10,1... | collective-permute-start | bytes 110600 | tf_op jit(solution)/shard_map/ppermute | solution.py:18
  24.0 19.4 %collective-permute-start.1 = (bf16[6,1,3072]{2,1,0:T(2,128)(2,1)S(1)}, bf16[6,1,3072]{2,1,0:T(2,128)(2,1)S(1)}, u32[]{:S(2)}, u32[]{:S(2)}) collective-permute-start(bf16[6,1,3072]{2,1,0:T(2,128)(2,1)S(1)} %get-tuple-element.115), channel_id=1, source_target_pairs={{1,0},{2,1},{3,2},{4,3},{5,4},{6,5},{7,6},{8,7},{9,8},{10,9},{11,1... | collective-permute-start | bytes 110600 | tf_op jit(solution)/shard_map/ppermute | solution.py:20
  37.3 6.1 %copy-start.5 = (bf16[6,1,3072]{2,1,0:T(2,128)(2,1)}, bf16[6,1,3072]{2,1,0:T(2,128)(2,1)S(1)}, u32[]{:S(2)}) copy-start(bf16[6,1,3072]{2,1,0:T(2,128)(2,1)S(1)} %collective-permute-done) | copy-start | bytes 110596
  52.7 14.3 %collective-permute-start.2 = (bf16[3,2,1,1024]{3,2,1,0:T(2,128)(2,1)S(1)}, bf16[3,2,1,1024]{3,2,1,0:T(2,128)(2,1)S(1)}, u32[]{:S(2)}, u32[]{:S(2)}) collective-permute-start(bf16[3,2,1,1024]{3,2,1,0:T(2,128)(2,1)S(1)} %get-tuple-element.119), channel_id=1, source_target_pairs={{0,1},{1,2},{2,3},{3,4},{4,5},{5,6},{6,7},{7,8},{8,9},{9,10},{10,1... | collective-permute-start | bytes 36872 | tf_op jit(solution)/shard_map/ppermute | solution.py:18
  64.1 21.8 %copy-start.44 = (s32[384]{0:T(512)S(1)}, s32[384]{0:T(512)}, u32[]{:S(2)}) copy-start(s32[384]{0:T(512)} %get-tuple-element.126) | copy-start | bytes 4612
  64.1 21.8 %copy-start.46 = (s32[384]{0:T(512)S(1)}, s32[384]{0:T(512)}, u32[]{:S(2)}) copy-start(s32[384]{0:T(512)} %get-tuple-element.135) | copy-start | bytes 4612
  64.1 21.8 %copy-start.56 = (f32[384]{0:T(512)S(1)}, f32[384]{0:T(512)}, u32[]{:S(2)}) copy-start(f32[384]{0:T(512)} %get-tuple-element.142) | copy-start | bytes 4612
  64.1 21.8 %copy-start.58 = (f32[384]{0:T(512)S(1)}, f32[384]{0:T(512)}, u32[]{:S(2)}) copy-start(f32[384]{0:T(512)} %get-tuple-element.150) | copy-start | bytes 4612
  64.1 21.8 %copy-start.74 = (s32[256]{0:T(256)S(1)}, s32[256]{0:T(256)}, u32[]{:S(2)}) copy-start(s32[256]{0:T(256)} %iota_add_fusion.5) | copy-start | bytes 3076
  64.1 18.7 %collective-permute-start.3 = (bf16[3,2,1,1024]{3,2,1,0:T(2,128)(2,1)S(1)}, bf16[3,2,1,1024]{3,2,1,0:T(2,128)(2,1)S(1)}, u32[]{:S(2)}, u32[]{:S(2)}) collective-permute-start(bf16[3,2,1,1024]{3,2,1,0:T(2,128)(2,1)S(1)} %get-tuple-element.120), channel_id=1, source_target_pairs={{1,0},{2,1},{3,2},{4,3},{5,4},{6,5},{7,6},{8,7},{9,8},{10,9},{11,1... | collective-permute-start | bytes 36872 | tf_op jit(solution)/shard_map/ppermute | solution.py:20
  66.9 19.5 %copy-start.36 = (s32[384]{0:T(512)S(1)}, s32[384]{0:T(512)}, u32[]{:S(2)}) copy-start(s32[384]{0:T(512)} %get-tuple-element.127) | copy-start | bytes 4612
  66.9 19.5 %copy-start.38 = (s32[384]{0:T(512)S(1)}, s32[384]{0:T(512)}, u32[]{:S(2)}) copy-start(s32[384]{0:T(512)} %get-tuple-element.134) | copy-start | bytes 4612
  67.0 19.5 %copy-start.48 = (f32[384]{0:T(512)S(1)}, f32[384]{0:T(512)}, u32[]{:S(2)}) copy-start(f32[384]{0:T(512)} %get-tuple-element.143) | copy-start | bytes 4612
  67.0 19.5 %copy-start.50 = (f32[384]{0:T(512)S(1)}, f32[384]{0:T(512)}, u32[]{:S(2)}) copy-start(f32[384]{0:T(512)} %get-tuple-element.149) | copy-start | bytes 4612
  67.0 19.5 %copy-start.70 = (s32[256]{0:T(256)S(1)}, s32[256]{0:T(256)}, u32[]{:S(2)}) copy-start(s32[256]{0:T(256)} %iota_add_fusion.4) | copy-start | bytes 3076
  84.7 2.2 %copy-start.28 = (s32[384]{0:T(512)S(1)}, s32[384]{0:T(512)}, u32[]{:S(2)}) copy-start(s32[384]{0:T(512)} %get-tuple-element.128) | copy-start | bytes 4612
  84.7 2.2 %copy-start.30 = (s32[384]{0:T(512)S(1)}, s32[384]{0:T(512)}, u32[]{:S(2)}) copy-start(s32[384]{0:T(512)} %get-tuple-element.133) | copy-start | bytes 4612
  84.7 2.2 %copy-start.40 = (f32[384]{0:T(512)S(1)}, f32[384]{0:T(512)}, u32[]{:S(2)}) copy-start(f32[384]{0:T(512)} %get-tuple-element.144) | copy-start | bytes 4612
  84.8 2.2 %copy-start.42 = (f32[384]{0:T(512)S(1)}, f32[384]{0:T(512)}, u32[]{:S(2)}) copy-start(f32[384]{0:T(512)} %get-tuple-element.148) | copy-start | bytes 4612
  84.8 2.2 %copy-start.68 = (s32[256]{0:T(256)S(1)}, s32[256]{0:T(256)}, u32[]{:S(2)}) copy-start(s32[256]{0:T(256)} %iota_add_fusion.3) | copy-start | bytes 3076
  85.9 1.5 %copy-start.20 = (s32[384]{0:T(512)S(1)}, s32[384]{0:T(512)}, u32[]{:S(2)}) copy-start(s32[384]{0:T(512)} %get-tuple-element.129) | copy-start | bytes 4612
  85.9 1.5 %copy-start.22 = (s32[384]{0:T(512)S(1)}, s32[384]{0:T(512)}, u32[]{:S(2)}) copy-start(s32[384]{0:T(512)} %get-tuple-element.132) | copy-start | bytes 4612
  85.9 1.5 %copy-start.32 = (f32[384]{0:T(512)S(1)}, f32[384]{0:T(512)}, u32[]{:S(2)}) copy-start(f32[384]{0:T(512)} %get-tuple-element.145) | copy-start | bytes 4612
  85.9 1.5 %copy-start.34 = (f32[384]{0:T(512)S(1)}, f32[384]{0:T(512)}, u32[]{:S(2)}) copy-start(f32[384]{0:T(512)} %get-tuple-element.147) | copy-start | bytes 4612
  85.9 1.5 %copy-start.66 = (s32[256]{0:T(256)S(1)}, s32[256]{0:T(256)}, u32[]{:S(2)}) copy-start(s32[256]{0:T(256)} %iota_add_fusion.2) | copy-start | bytes 3076
  86.4 1.5 %copy-start.12 = (s32[384]{0:T(512)S(1)}, s32[384]{0:T(512)}, u32[]{:S(2)}) copy-start(s32[384]{0:T(512)} %get-tuple-element.130) | copy-start | bytes 4612
  86.4 1.5 %copy-start.14 = (s32[384]{0:T(512)S(1)}, s32[384]{0:T(512)}, u32[]{:S(2)}) copy-start(s32[384]{0:T(512)} %get-tuple-element.138) | copy-start | bytes 4612
  86.4 1.5 %copy-start.24 = (f32[384]{0:T(512)S(1)}, f32[384]{0:T(512)}, u32[]{:S(2)}) copy-start(f32[384]{0:T(512)} %get-tuple-element.146) | copy-start | bytes 4612
  86.4 1.5 %copy-start.26 = (f32[384]{0:T(512)S(1)}, f32[384]{0:T(512)}, u32[]{:S(2)}) copy-start(f32[384]{0:T(512)} %get-tuple-element.154) | copy-start | bytes 4612
  95.1 1.5 %copy-start.1 = (f32[5,12,3072]{2,1,0:T(8,128)S(1)}, f32[5,12,3072]{2,1,0:T(8,128)}, u32[]{:S(2)}) copy-start(f32[5,12,3072]{2,1,0:T(8,128)} %get-tuple-element.107) | copy-start | bytes 2211844
  95.1 1.5 %copy-start.7 = (f32[3072]{0:T(1024)S(1)}, f32[3072]{0:T(1024)}, u32[]{:S(2)}) copy-start(f32[3072]{0:T(1024)} %param.25) | copy-start | bytes 36868
  95.1 1.5 %copy-start.8 = (f32[3072]{0:T(1024)S(1)}, f32[3072]{0:T(1024)}, u32[]{:S(2)}) copy-start(f32[3072]{0:T(1024)} %get-tuple-element.99) | copy-start | bytes 36868
  95.1 1.5 %copy-start.9 = (f32[3072]{0:T(1024)S(1)}, f32[3072]{0:T(1024)}, u32[]{:S(2)}) copy-start(f32[3072]{0:T(1024)} %get-tuple-element.100) | copy-start | bytes 36868
  101.2 2.3 %copy-start.45 = (s32[384]{0:T(512)S(1)}, s32[384]{0:T(512)}, u32[]{:S(2)}) copy-start(s32[384]{0:T(512)} %get-tuple-element.126) | copy-start | bytes 4612
  101.2 2.3 %copy-start.47 = (s32[384]{0:T(512)S(1)}, s32[384]{0:T(512)}, u32[]{:S(2)}) copy-start(s32[384]{0:T(512)} %get-tuple-element.135) | copy-start | bytes 4612
  101.2 2.3 %copy-start.57 = (f32[384]{0:T(512)S(1)}, f32[384]{0:T(512)}, u32[]{:S(2)}) copy-start(f32[384]{0:T(512)} %get-tuple-element.142) | copy-start | bytes 4612
  101.2 2.3 %copy-start.59 = (f32[384]{0:T(512)S(1)}, f32[384]{0:T(512)}, u32[]{:S(2)}) copy-start(f32[384]{0:T(512)} %get-tuple-element.150) | copy-start | bytes 4612
  101.2 2.3 %copy-start.75 = (s32[256]{0:T(256)S(1)}, s32[256]{0:T(256)}, u32[]{:S(2)}) copy-start(s32[256]{0:T(256)} %iota_add_fusion.5) | copy-start | bytes 3076
  101.7 3.1 %copy-start.37 = (s32[384]{0:T(512)S(1)}, s32[384]{0:T(512)}, u32[]{:S(2)}) copy-start(s32[384]{0:T(512)} %get-tuple-element.127) | copy-start | bytes 4612
  101.7 3.1 %copy-start.39 = (s32[384]{0:T(512)S(1)}, s32[384]{0:T(512)}, u32[]{:S(2)}) copy-start(s32[384]{0:T(512)} %get-tuple-element.134) | copy-start | bytes 4612
  101.7 3.1 %copy-start.49 = (f32[384]{0:T(512)S(1)}, f32[384]{0:T(512)}, u32[]{:S(2)}) copy-start(f32[384]{0:T(512)} %get-tuple-element.143) | copy-start | bytes 4612
  101.7 3.1 %copy-start.51 = (f32[384]{0:T(512)S(1)}, f32[384]{0:T(512)}, u32[]{:S(2)}) copy-start(f32[384]{0:T(512)} %get-tuple-element.149) | copy-start | bytes 4612
  101.7 3.1 %copy-start.71 = (s32[256]{0:T(256)S(1)}, s32[256]{0:T(256)}, u32[]{:S(2)}) copy-start(s32[256]{0:T(256)} %iota_add_fusion.4) | copy-start | bytes 3076
  102.3 3.6 %copy-start.29 = (s32[384]{0:T(512)S(1)}, s32[384]{0:T(512)}, u32[]{:S(2)}) copy-start(s32[384]{0:T(512)} %get-tuple-element.128) | copy-start | bytes 4612
  102.3 3.6 %copy-start.31 = (s32[384]{0:T(512)S(1)}, s32[384]{0:T(512)}, u32[]{:S(2)}) copy-start(s32[384]{0:T(512)} %get-tuple-element.133) | copy-start | bytes 4612
  102.3 3.6 %copy-start.41 = (f32[384]{0:T(512)S(1)}, f32[384]{0:T(512)}, u32[]{:S(2)}) copy-start(f32[384]{0:T(512)} %get-tuple-element.144) | copy-start | bytes 4612
  102.4 3.6 %copy-start.43 = (f32[384]{0:T(512)S(1)}, f32[384]{0:T(512)}, u32[]{:S(2)}) copy-start(f32[384]{0:T(512)} %get-tuple-element.148) | copy-start | bytes 4612
  102.4 3.6 %copy-start.69 = (s32[256]{0:T(256)S(1)}, s32[256]{0:T(256)}, u32[]{:S(2)}) copy-start(s32[256]{0:T(256)} %iota_add_fusion.3) | copy-start | bytes 3076
  102.9 4.1 %copy-start.21 = (s32[384]{0:T(512)S(1)}, s32[384]{0:T(512)}, u32[]{:S(2)}) copy-start(s32[384]{0:T(512)} %get-tuple-element.129) | copy-start | bytes 4612
  102.9 4.1 %copy-start.23 = (s32[384]{0:T(512)S(1)}, s32[384]{0:T(512)}, u32[]{:S(2)}) copy-start(s32[384]{0:T(512)} %get-tuple-element.132) | copy-start | bytes 4612
  102.9 4.1 %copy-start.33 = (f32[384]{0:T(512)S(1)}, f32[384]{0:T(512)}, u32[]{:S(2)}) copy-start(f32[384]{0:T(512)} %get-tuple-element.145) | copy-start | bytes 4612
  103.0 4.1 %copy-start.35 = (f32[384]{0:T(512)S(1)}, f32[384]{0:T(512)}, u32[]{:S(2)}) copy-start(f32[384]{0:T(512)} %get-tuple-element.147) | copy-start | bytes 4612
  103.0 4.1 %copy-start.67 = (s32[256]{0:T(256)S(1)}, s32[256]{0:T(256)}, u32[]{:S(2)}) copy-start(s32[256]{0:T(256)} %iota_add_fusion.2) | copy-start | bytes 3076
  104.1 4.0 %copy-start.13 = (s32[384]{0:T(512)S(1)}, s32[384]{0:T(512)}, u32[]{:S(2)}) copy-start(s32[384]{0:T(512)} %get-tuple-element.130) | copy-start | bytes 4612
  104.1 4.0 %copy-start.15 = (s32[384]{0:T(512)S(1)}, s32[384]{0:T(512)}, u32[]{:S(2)}) copy-start(s32[384]{0:T(512)} %get-tuple-element.138) | copy-start | bytes 4612
  104.1 4.0 %copy-start.25 = (f32[384]{0:T(512)S(1)}, f32[384]{0:T(512)}, u32[]{:S(2)}) copy-start(f32[384]{0:T(512)} %get-tuple-element.146) | copy-start | bytes 4612
  104.2 4.0 %copy-start.27 = (f32[384]{0:T(512)S(1)}, f32[384]{0:T(512)}, u32[]{:S(2)}) copy-start(f32[384]{0:T(512)} %get-tuple-element.154) | copy-start | bytes 4612
  104.2 4.0 %copy-start.65 = (s32[256]{0:T(256)S(1)}, s32[256]{0:T(256)}, u32[]{:S(2)}) copy-start(s32[256]{0:T(256)} %iota_add_fusion.1) | copy-start | bytes 3076
  105.3 3.9 %copy-start.11 = (s32[384]{0:T(512)S(1)}, s32[384]{0:T(512)}, u32[]{:S(2)}) copy-start(s32[384]{0:T(512)} %get-tuple-element.131) | copy-start | bytes 4612
  105.3 3.9 %copy-start.17 = (f32[384]{0:T(512)S(1)}, f32[384]{0:T(512)}, u32[]{:S(2)}) copy-start(f32[384]{0:T(512)} %get-tuple-element.139) | copy-start | bytes 4612
  105.3 3.9 %copy-start.19 = (f32[384]{0:T(512)S(1)}, f32[384]{0:T(512)}, u32[]{:S(2)}) copy-start(f32[384]{0:T(512)} %get-tuple-element.153) | copy-start | bytes 4612
  105.3 3.9 %copy-start.73 = (s32[256]{0:T(256)S(1)}, s32[256]{0:T(256)}, u32[]{:S(2)}) copy-start(s32[256]{0:T(256)} %iota_add_fusion) | copy-start | bytes 3076
  (18 other events, 19.3 us)
where the time goes:
time: 134 us; the launch traced here: 133 us
  starting transfers between devices  35.7 us (27%)
  local copies, waits for them, and re-layouts  25.2 us (19%)
  waiting for transfers between devices  21.9 us (16%)
  blocking collectives  20.1 us (15%)
  other arithmetic  19.7 us (15%)
  matrix products  8.69 us (6%)
  between operations  2.12 us (2%)
    ppermute x2, waiting for transfers between devices, padded(): lax.ppermute(head, axis, [((i + 1) % count, i) for i in range(count)])  21.9 us
    all_to_all x1, blocking collectives, body(): lax.all_to_all(restricted[:, None], 'wn', split_axis=3, concat_axis=1, ti...  20.1 us
    ppermute x2, starting transfers between devices, padded(): lax.ppermute(tail, axis, [(i, (i + 1) % count) for i in range(count)])  19.2 us
    all_to_all x1, starting transfers between devices, body(): lax.all_to_all(velocity, 'wn', split_axis=2, concat_axis=4, tiled=True)  12.7 us
    unnamed x159, local copies, waits for them, and re-layouts  7.47 us
    dot_general x8, matrix products, wall_interpolate(): jnp.einsum('cpyk,kj->cpyj', values[..., start:start + window], matrix, pr...  4.53 us
    dot_general x8, matrix products, wall_restrict(): jnp.einsum('pyj,kj->pyk', part, matrix, precision=lax.Precision.HIGHEST)  4.16 us
    add x7, other arithmetic, weight_block(): rows = start + jnp.arange(window, dtype=jnp.int32)  4.07 us
  transfers between devices with their start and end apart: 5, of which 2 were waited for; matrix products, arithmetic and copies ran while one was open for 12% of the time, Pallas kernels for 0%

commit v1 on v0

v1 whole, which is shorter than its diff:
```python
import numpy as np
import jax
import jax.numpy as jnp
from jax import lax
from jax.experimental import pallas as pl
from jax.experimental.pallas import tpu as pltpu
from jax.sharding import PartitionSpec as P

TIME_STEP = 0.5
RUNGE_GAMMA = 8.0 / 15.0
DIFFUSIVITY = 0.3

PLANES = 6
ROWS = 12
FINE = 3072
COARSE = 1024
OWNERS = 16
SLAB = 64
BLOCK = 128
BLOCKS = FINE // BLOCK
WINDOW = 256
STACK = 32
HALO_ROWS = 24
CHUNK = 512

f32 = jnp.float32
bf16 = jnp.bfloat16
SCALE = TIME_STEP * RUNGE_GAMMA
FLAT = SCALE * DIFFUSIVITY
SIDE = 0.5 * SCALE / 9.0

ACROSS = [[(1 - plane // 3, 1), (plane // 3, 2)] if plane % 3 == 0 else [(plane // 3, 3)] if plane % 3 == 1 else [(plane // 3, 2), (1 - plane // 3, 1)] for plane in range(PLANES)]
ALONG = [[(row // 3 - 1, 1), (row // 3, 2)] if row % 3 == 0 else [(row // 3, 3)] if row % 3 == 1 else [(row // 3, 2), (row // 3 + 1, 1)] for row in range(ROWS)]


def own_matrix():
    matrix = np.zeros((3, PLANES, 16, STACK), np.float32)
    for c in range(3):
        for plane in range(PLANES):
            for row in range(ROWS):
                for p, a in ACROSS[plane]:
                    for m, b in ALONG[row]:
                        if 0 <= m < 4:
                            matrix[c, plane, row, p * 16 + c * 4 + m] += a * b
    matrix = matrix.reshape(3 * PLANES * 16, STACK)
    return np.concatenate([matrix, matrix], axis=1)


def side_matrix():
    matrix = np.zeros((3, 8, 8), np.float32)
    for c in range(3):
        for plane in range(PLANES):
            for p, a in ACROSS[plane]:
                matrix[c, plane, p * 3 + c] += a
    matrix = matrix.reshape(24, 8)
    return np.concatenate([matrix, matrix], axis=1)


def group_matrices():
    inner = np.zeros((8, PLANES, 16), np.float32)
    outer = np.zeros((8, 8), np.float32)
    for p in range(2):
        for y in range(4):
            inner[p * 4 + y, 3 * p : 3 * p + 3, 3 * y : 3 * y + 3] = 1.0
        inner[:, :, 0] = 0.0
        inner[:, :, ROWS - 1] = 0.0
        outer[p, 3 * p : 3 * p + 3] = 1.0
    return inner.reshape(8, PLANES * 16), outer


OWN_MATRIX = own_matrix()
SIDE_MATRIX = side_matrix()
INNER_GROUPS, OUTER_GROUPS = group_matrices()


def bundle():
    matrix = np.zeros((368, 128), np.float32)
    for first, part in ((0, OWN_MATRIX), (288, INNER_GROUPS), (304, SIDE_MATRIX), (352, OUTER_GROUPS)):
        matrix[first : first + part.shape[0], : part.shape[1]] = part
    return matrix


BUNDLE = bundle()


def window_starts(wall_index):
    starts = []
    for b in range(BLOCKS):
        first = jnp.min(wall_index[b : b + 1, :])
        starts.append(pl.multiple_of(jnp.minimum(lax.shift_right_logical(first, 7) * 128, COARSE - WINDOW), 128))
    return starts


def load_kernel(
    velocity_hbm, salinity_hbm, index_hbm, weight_hbm, spacing_hbm, matrices_hbm,
    send, salinity, index, weight, spacing, matrices, velocity, copied,
):
    copies = [
        pltpu.make_async_copy(source, target, copied.at[number])
        for number, (source, target) in enumerate(
            (
                (velocity_hbm, velocity),
                (salinity_hbm, salinity),
                (index_hbm, index),
                (weight_hbm, weight),
                (spacing_hbm, spacing),
                (matrices_hbm, matrices),
            )
        )
    ]
    for copy in copies:
        copy.start()
    copies[0].wait()
    for q in range(OWNERS):
        for c in range(3):
            for p in range(2):
                send[q, :, c * 128 + p * 64 : c * 128 + p * 64 + 64] = velocity[c, p, q]
    for copy in copies[1:]:
        copy.wait()


def edge_kernel(salinity, arrived, second, first, coarse):
    odd = lax.rem(lax.axis_index("sw"), 2)
    left = lax.broadcasted_iota(jnp.int32, (4, 128), 1) < 64
    for t in range(8):
        lanes = slice(t * 128, t * 128 + 128)
        for c in range(3):
            one = arrived[2 * t, :, c * 128 : c * 128 + 128].astype(f32)
            two = arrived[2 * t + 1, :, c * 128 : c * 128 + 128].astype(f32)
            coarse[c * 4 : c * 4 + 4, lanes] = jnp.where(left, one, pltpu.roll(two, 64, 1))
            coarse[16 + c * 4 : 20 + c * 4, lanes] = jnp.where(left, pltpu.roll(one, 64, 1), two)
    coarse[12:16, :] = jnp.zeros((4, COARSE), f32)
    coarse[28:32, :] = jnp.zeros((4, COARSE), f32)
    for part in range(3):
        lanes = slice(part * 1024, part * 1024 + 1024)
        head = salinity[:, 0, lanes].astype(f32)
        tail = salinity[:, ROWS - 1, lanes].astype(f32)
        second[part * 6 : part * 6 + 6, :] = jnp.where(odd > 0, tail, head).astype(bf16)
        first[part * 6 : part * 6 + 6, :] = jnp.where(odd > 0, head, tail).astype(bf16)
    head = jnp.concatenate([coarse[p * 16 + c * 4 : p * 16 + c * 4 + 1, :] for p in range(2) for c in range(3)], axis=0)
    tail = jnp.concatenate([coarse[p * 16 + c * 4 + 3 : p * 16 + c * 4 + 4, :] for p in range(2) for c in range(3)], axis=0)
    second[18:24, :] = jnp.where(odd > 0, tail, head).astype(bf16)
    first[18:24, :] = jnp.where(odd > 0, head, tail).astype(bf16)


def inner_kernel(
    salinity, coarse, wall_index, wall_weight, spacing, matrices,
    updated, edges, grouped, hits, turned_hits, field, factors, sources, normal,
):
    width = spacing[...]
    before = pltpu.roll(width, 1, 1)
    after = pltpu.roll(width, FINE - 1, 1)
    column = lax.broadcasted_iota(jnp.int32, (1, FINE), 1)
    gap_low = jnp.where(column == 0, width, 0.5 * (before + width))
    gap_high = jnp.where(column == FINE - 1, width, 0.5 * (width + after))
    factors[0:1, :] = FLAT / (gap_high * width)
    factors[1:2, :] = FLAT / (gap_low * width)
    factors[2:3, :] = (SCALE / 9.0) / (gap_low + gap_high)

    for plane in range(PLANES):
        field[plane, 0:ROWS, :] = salinity[plane].astype(f32)
        field[plane, ROWS:16, :] = jnp.zeros((16 - ROWS, FINE), f32)

    starts = window_starts(wall_index)
    whole = coarse[...]
    sources[0:STACK, :] = whole.astype(bf16)
    sources[STACK : 2 * STACK, :] = pltpu.roll(whole, COARSE - 1, 1).astype(bf16)
    table = jnp.concatenate([wall_index[...].astype(f32), jnp.zeros((128 - BLOCKS, BLOCK), f32)], axis=0)
    columns = table.T.astype(jnp.int32)
    cell = lax.broadcasted_iota(jnp.int32, (WINDOW, BLOCK), 0)
    turned_cell = lax.broadcasted_iota(jnp.int32, (BLOCK, WINDOW), 1)
    for b in range(BLOCKS):
        lanes = slice(b * BLOCK, b * BLOCK + BLOCK)
        hit = jnp.where(cell == wall_index[b : b + 1, :] - starts[b], 1.0, 0.0).astype(bf16)
        hits[b] = hit
        turned_hits[b] = jnp.where(turned_cell == columns[:, b : b + 1] - starts[b], 1.0, 0.0).astype(bf16)
        both = jnp.dot(sources[:, pl.ds(starts[b], WINDOW)], hit, preferred_element_type=f32)
        weight = wall_weight[:, lanes]
        value = (1.0 - weight) * both[0:STACK] + weight * both[STACK : 2 * STACK]
        upper = value.astype(bf16)
        normal[0:STACK, lanes] = upper
        normal[STACK : 2 * STACK, lanes] = (value - upper.astype(f32)).astype(bf16)

    lane = lax.broadcasted_iota(jnp.int32, (16, BLOCK), 1)
    for b in range(BLOCKS):
        lanes = slice(b * BLOCK, b * BLOCK + BLOCK)
        velocity = jnp.dot(matrices[0:288, 0:64], normal[:, lanes], preferred_element_type=f32)
        up = factors[0:1, lanes]
        down = factors[1:2, lanes]
        slant = factors[2:3, lanes]
        block = [field[plane, :, lanes] for plane in range(PLANES)]
        results = []
        for plane in range(PLANES):
            here = block[plane]
            if b == 0:
                low_side = -here[:, 0:1]
            else:
                low_side = pltpu.roll(field[plane, :, (b - 1) * BLOCK : b * BLOCK], 1, 1)
            if b == BLOCKS - 1:
                high_side = -here[:, BLOCK - 1 : BLOCK]
            else:
                high_side = pltpu.roll(field[plane, :, (b + 1) * BLOCK : (b + 2) * BLOCK], BLOCK - 1, 1)
            wall_low = jnp.where(lane == 0, low_side, pltpu.roll(here, 1, 1))
            wall_high = jnp.where(lane == BLOCK - 1, high_side, pltpu.roll(here, BLOCK - 1, 1))
            forward = pltpu.roll(here, 15, 0)
            behind = pltpu.roll(here, 1, 0)
            span_low = block[(plane - 1) % PLANES]
            span_high = block[(plane + 1) % PLANES]
            u = velocity[plane * 16 : plane * 16 + 16]
            v = velocity[96 + plane * 16 : 96 + plane * 16 + 16]
            w = velocity[192 + plane * 16 : 192 + plane * 16 + 16]
            along = SIDE * (forward - behind)
            slope = (wall_high - wall_low) * slant
            across = SIDE * (span_high - span_low)
            new = here + (wall_high - here) * up - (here - wall_low) * down
            new = new + FLAT * ((forward + behind) + (span_high + span_low) - 4.0 * here)
            new = new - (u * along + v * slope + w * across)
            for number, value in enumerate((new, u, along, slope, across)):
                edges[number, plane : plane + 1, lanes] = value[0:1]
                edges[number, 8 + plane : 9 + plane, lanes] = value[ROWS - 1 : ROWS]
            new = new.astype(bf16)
            updated[plane, :, lanes] = new[0:ROWS]
            results.append(new)
        stacked = jnp.concatenate(results, axis=0)
        grouped[:, lanes] = jnp.dot(matrices[288:296, 0:96], stacked, preferred_element_type=f32)


def edge_row(message, base, sign, edges, hits, starts, wall_weight, matrices, sources, raw, normal):
    column = message[18:24, :].astype(f32)
    spare = jnp.zeros((2, COARSE), f32)
    column = jnp.concatenate([column, spare], axis=0)
    sources[0:16, :] = jnp.concatenate([column, pltpu.roll(column, COARSE - 1, 1)], axis=0).astype(bf16)
    for b in range(BLOCKS):
        lanes = slice(b * BLOCK, b * BLOCK + BLOCK)
        raw[:, lanes] = jnp.dot(sources[:, pl.ds(starts[b], WINDOW)], hits[b], preferred_element_type=f32)
    results = []
    spare = jnp.zeros((2, CHUNK), f32)
    for k in range(FINE // CHUNK):
        lanes = slice(k * CHUNK, k * CHUNK + CHUNK)
        weight = wall_weight[:, lanes]
        value = (1.0 - weight) * raw[0:8, lanes] + weight * raw[8:16, lanes]
        upper = value.astype(bf16).astype(f32)
        normal[:, lanes] = jnp.concatenate([upper, value - upper], axis=0).astype(bf16)
        velocity = jnp.dot(matrices[304:328, 0:16], normal[:, lanes], preferred_element_type=f32)
        part, offset = divmod(k * CHUNK, 1024)
        ghost = message[part * 6 : part * 6 + 6, offset : offset + CHUNK].astype(f32)
        ghost = jnp.concatenate([ghost, spare], axis=0)
        pull = sign * ghost
        at = pl.ds(base, 8)
        new = edges[0, at, lanes] + FLAT * ghost + edges[1, at, lanes] * pull
        new = new + velocity[0:8] * (pull - edges[2, at, lanes])
        new = new - velocity[8:16] * edges[3, at, lanes] - velocity[16:24] * edges[4, at, lanes]
        results.append(new.astype(bf16))
    return results


def split_terms(sums, weight):
    sums = sums * (1.0 / 9.0)
    above = sums * weight
    below = sums - above
    below_upper = below.astype(bf16).astype(f32)
    above_upper = above.astype(bf16).astype(f32)
    return jnp.concatenate([below_upper, below - below_upper, above_upper, above - above_upper], axis=0).astype(bf16)


def near_kernel(
    message, inner, edges, grouped, hits, turned_hits, wall_index, wall_weight, matrices,
    updated, sums, total, sources, raw, normal, terms, parts,
):
    odd = lax.rem(lax.axis_index("sw"), 2)
    starts = window_starts(wall_index)
    base = pl.multiple_of(8 * (1 - odd), 8)
    sign = jnp.where(odd > 0, SIDE, -SIDE)
    edge = jnp.where(odd > 0, 0, ROWS - 1)
    rows = edge_row(message, base, sign, edges, hits, starts, wall_weight, matrices, sources, raw, normal)
    own = lax.broadcasted_iota(jnp.int32, (8, CHUNK), 0)
    far = jnp.where(odd > 0, 3, 0)
    row = lax.broadcasted_iota(jnp.int32, (ROWS, CHUNK), 0)
    for k, rounded in enumerate(rows):
        lanes = slice(k * CHUNK, k * CHUNK + CHUNK)
        added = jnp.dot(matrices[352:360, 0:8], rounded, preferred_element_type=f32)
        near = 3 - far
        low = jnp.where(own == near, added[0:1], jnp.where(own == near + 4, added[1:2], 0.0))
        whole = grouped[:, lanes] + low
        waiting = jnp.logical_or(own == far, own == far + 4)
        late = jnp.where(waiting, whole, 0.0)
        sums[:, lanes] = jnp.concatenate(
            [jnp.sum(late[0:4], axis=0, keepdims=True), jnp.sum(late[4:8], axis=0, keepdims=True), jnp.zeros((6, CHUNK), f32)],
            axis=0,
        )
        terms[:, lanes] = split_terms(whole - late, wall_weight[:, lanes])
        new = rounded.astype(f32)
        for plane in range(PLANES):
            kept = jnp.where(row == edge, new[plane : plane + 1], inner[plane, :, lanes].astype(f32))
            updated[plane, :, lanes] = kept.astype(bf16)
    for b in range(BLOCKS):
        lanes = slice(b * BLOCK, b * BLOCK + BLOCK)
        parts[b] = jnp.dot(terms[:, lanes], turned_hits[b], preferred_element_type=f32)
    total[...] = jnp.zeros_like(total)
    for b in range(BLOCKS):
        part = parts[b]
        total[0:8, pl.ds(starts[b], WINDOW)] += part[0:8] + part[8:16]
        total[8:16, pl.ds(starts[b], WINDOW)] += part[16:24] + part[24:32]


def far_kernel(
    message, near, sums, near_total, edges, hits, turned_hits, wall_index, wall_weight, matrices,
    updated_hbm, send, sources, raw, normal, terms, parts, total, updated, copied,
):
    odd = lax.rem(lax.axis_index("sw"), 2)
    starts = window_starts(wall_index)
    base = pl.multiple_of(8 * odd, 8)
    sign = jnp.where(odd > 0, -SIDE, SIDE)
    edge = jnp.where(odd > 0, ROWS - 1, 0)
    rows = edge_row(message, base, sign, edges, hits, starts, wall_weight, matrices, sources, raw, normal)
    chunks = [slice(k * CHUNK, k * CHUNK + CHUNK) for k in range(FINE // CHUNK)]
    row = lax.broadcasted_iota(jnp.int32, (ROWS, CHUNK), 0)
    copies = []
    for plane in range(PLANES):
        for lanes, rounded in zip(chunks, rows):
            new = rounded[plane : plane + 1].astype(f32)
            updated[plane, :, lanes] = jnp.where(row == edge, new, near[plane, :, lanes].astype(f32)).astype(bf16)
        copy = pltpu.make_async_copy(updated.at[plane], updated_hbm.at[plane], copied.at[plane])
        copy.start()
        copies.append(copy)

    spare = jnp.zeros((8, CHUNK), bf16)
    for lanes, rounded in zip(chunks, rows):
        whole = sums[:, lanes] + jnp.dot(matrices[352:360, 0:8], rounded, preferred_element_type=f32)
        terms[:, lanes] = jnp.concatenate([split_terms(whole[0:2], wall_weight[:, lanes]), spare], axis=0)
    for b in range(BLOCKS):
        lanes = slice(b * BLOCK, b * BLOCK + BLOCK)
        parts[b] = jnp.dot(terms[:, lanes], turned_hits[b], preferred_element_type=f32)[0:8]

    total[...] = jnp.zeros_like(total)
    for b in range(BLOCKS):
        total[:, pl.ds(starts[b], WINDOW)] += parts[b]
    last = lax.broadcasted_iota(jnp.int32, (8, COARSE), 1)
    own = lax.broadcasted_iota(jnp.int32, (8, COARSE), 0)
    far = jnp.where(odd > 0, 3, 0)
    below = total[0:2] + total[2:4]
    above = total[4:6] + total[6:8]
    below = jnp.where(own == far, below[0:1], jnp.where(own == far + 4, below[1:2], near_total[0:8, :]))
    above = jnp.where(own == far, above[0:1], jnp.where(own == far + 4, above[1:2], near_total[8:16, :]))
    restricted = below + jnp.where(last == 0, 0.0, pltpu.roll(above, 1, 1))
    left = lax.broadcasted_iota(jnp.int32, (4, 128), 1) < 64
    for t in range(8):
        tile = restricted[:, t * 128 : t * 128 + 128]
        turned = pltpu.roll(tile, 64, 1)
        send[2 * t] = jnp.where(left, tile[0:4], turned[4:8]).astype(bf16)
        send[2 * t + 1] = jnp.where(left, turned[0:4], tile[4:8]).astype(bf16)
    for copy in copies:
        copy.wait()


def spread_kernel(arrived, coarse):
    for q in range(OWNERS):
        for p in range(2):
            coarse[p, q] = arrived[q, :, p * 64 : p * 64 + 64]


VMEM = pl.BlockSpec(memory_space=pltpu.VMEM)
ANY = pl.BlockSpec(memory_space=pl.ANY)


def call(kernel, shapes, in_specs, scratch=(), megabytes=16, cost=None, out_specs=None):
    single = not isinstance(shapes, list)
    return pl.pallas_call(
        kernel,
        out_shape=shapes,
        in_specs=in_specs,
        out_specs=out_specs or (VMEM if single else [VMEM] * len(shapes)),
        scratch_shapes=list(scratch),
        cost_estimate=cost,
        compiler_params=pltpu.CompilerParams(vmem_limit_bytes=megabytes * 1024 * 1024),
    )


def body(salinity, velocity, wall_index, wall_weight, spacing):
    total_count = lax.axis_size("sw") * lax.axis_size("wn")
    near = [(i, i ^ 1) for i in range(total_count)]
    far = []
    for i in range(total_count):
        far.append((i, (i + 1) % total_count if i % 2 else (i - 1) % total_count))

    matrices = jnp.asarray(BUNDLE, bf16)
    message = jax.ShapeDtypeStruct((HALO_ROWS, COARSE), bf16)
    fine = jax.ShapeDtypeStruct((PLANES, ROWS, FINE), bf16)
    own, salinity, wall_index, wall_weight, spacing, matrices = call(
        load_kernel,
        [
            pltpu.VMEM((OWNERS, 4, 384), bf16),
            pltpu.VMEM((PLANES, ROWS, FINE), bf16),
            pltpu.VMEM((BLOCKS, BLOCK), jnp.int32),
            pltpu.VMEM((1, FINE), f32),
            pltpu.VMEM((1, FINE), f32),
            pltpu.VMEM((368, 128), bf16),
        ],
        [ANY] * 6,
        [pltpu.VMEM((3, 2, OWNERS, 4, SLAB), bf16), pltpu.SemaphoreType.DMA((6,))],
        megabytes=56,
    )(velocity, salinity, wall_index.reshape(BLOCKS, BLOCK), wall_weight[None], spacing[None], matrices)
    arrived = lax.all_to_all(own, "wn", split_axis=0, concat_axis=0, tiled=True)
    second, first, coarse = call(
        edge_kernel, [message, message, jax.ShapeDtypeStruct((STACK, COARSE), f32)], [VMEM] * 2
    )(salinity, arrived)
    second_in = lax.ppermute(second, ("wn", "sw"), far)
    first_in = lax.ppermute(first, ("wn", "sw"), near)
    inner = call(
        inner_kernel,
        [
            fine,
            jax.ShapeDtypeStruct((5, 16, FINE), f32),
            jax.ShapeDtypeStruct((8, FINE), f32),
            jax.ShapeDtypeStruct((BLOCKS, WINDOW, BLOCK), bf16),
            jax.ShapeDtypeStruct((BLOCKS, BLOCK, WINDOW), bf16),
        ],
        [VMEM] * 6,
        [
            pltpu.VMEM((PLANES, 16, FINE), f32),
            pltpu.VMEM((8, FINE), f32),
            pltpu.VMEM((2 * STACK, COARSE), bf16),
            pltpu.VMEM((2 * STACK, FINE), bf16),
        ],
        cost=pl.CostEstimate(flops=4_000_000_000, bytes_accessed=2_000_000_000, transcendentals=0),
    )(
        salinity, coarse, wall_index, wall_weight, spacing, matrices,
    )
    interior, edges, grouped, hits, turned_hits = inner
    work = [
        pltpu.VMEM((16, COARSE), bf16),
        pltpu.VMEM((16, FINE), f32),
        pltpu.VMEM((16, FINE), bf16),
    ]
    near_updated, sums, near_total = call(
        near_kernel,
        [fine, jax.ShapeDtypeStruct((8, FINE), f32), jax.ShapeDtypeStruct((16, COARSE), f32)],
        [VMEM] * 9,
        work + [pltpu.VMEM((32, FINE), bf16), pltpu.VMEM((BLOCKS, 32, WINDOW), f32)],
        cost=pl.CostEstimate(flops=1000, bytes_accessed=1000, transcendentals=0),
    )(first_in, interior, edges, grouped, hits, turned_hits, wall_index, wall_weight, matrices)
    updated, send = call(
        far_kernel,
        [fine, jax.ShapeDtypeStruct((OWNERS, 4, 128), bf16)],
        [VMEM] * 10,
        work
        + [
            pltpu.VMEM((16, FINE), bf16),
            pltpu.VMEM((BLOCKS, 8, WINDOW), f32),
            pltpu.VMEM((8, COARSE), f32),
            pltpu.VMEM((PLANES, ROWS, FINE), bf16),
            pltpu.SemaphoreType.DMA((PLANES,)),
        ],
        out_specs=[ANY, VMEM],
    )(second_in, near_updated, sums, near_total, edges, hits, turned_hits, wall_index, wall_weight, matrices)
    back = lax.all_to_all(send, "wn", split_axis=0, concat_axis=0, tiled=True)
    coarse = call(spread_kernel, jax.ShapeDtypeStruct((2, OWNERS, 4, SLAB), bf16), [VMEM])(back)
    return (updated, coarse)


def solution(mesh):
    in_specs = (P(None, ("wn", "sw"), None), P(None, None, None, "sw", "wn"), P(), P(), P())
    out_specs = (P(None, ("wn", "sw"), None), P(None, None, "sw", "wn"))
    return jax.shard_map(body, mesh=mesh, in_specs=in_specs, out_specs=out_specs, check_vma=False)
```

time: 134 us -> 63.1 us (0.47)
  starting transfers between devices: 35.7 us -> 9.71 us
  local copies, waits for them, and re-layouts: 25.2 us -> 0 us
  other arithmetic: 19.7 us -> 0 us
  waiting for transfers between devices: 21.9 us -> 4.28 us
  blocking collectives: 20.1 us -> 37.6 us
  Pallas kernels: 0 us -> 10.6 us
  matrix products: 8.69 us -> 0 us
  between operations: 2.12 us -> 0.67 us
    ppermute x4 -> x2, waiting for transfers between devices: 21.9 us -> 4.28 us  [the longest x1 4.27 us: body(): second_in = lax.ppermute(second, ('wn', 'sw'), far)]
    all_to_all x1 -> x2, blocking collectives: 20.1 us -> 37.6 us  [the longest x1 23.2 us: body(): arrived = lax.all_to_all(own, 'wn', split_axis=0, concat_axis=0, tiled=True)]
    ppermute x4 -> x2, starting transfers between devices: 23 us -> 9.71 us  [the longest x1 7.79 us: body(): second_in = lax.ppermute(second, ('wn', 'sw'), far)]
    all_to_all x1 -> x0, starting transfers between devices: 12.7 us -> none  [body(): lax.all_to_all(velocity, 'wn', split_axis=2, concat_axis=4, tiled=True)]
    pallas_call x0 -> x6, Pallas kernels: none -> 10.6 us  [the longest x1 5.17 us: body(): call(inner_kernel, [fine, jax.ShapeDtypeStruct((5, 16, FINE), f32), jax.S...]
    dot_general x16 -> x0, matrix products: 8.69 us -> none  [the longest x8 4.53 us: wall_interpolate(): jnp.einsum('cpyk,kj->cpyj', values[..., start:start + window], matrix, pr...]
    unnamed x159 -> x0, local copies, waits for them, and re-layouts: 7.47 us -> none
    add x9 -> x0, other arithmetic: 7.45 us -> none  [the longest x7 4.07 us: weight_block(): rows = start + jnp.arange(window, dtype=jnp.int32)]
  transfers between devices with their start and end apart: 5 -> 2, of which waited for: 2 -> 1; matrix products, arithmetic and copies ran while one was open for 12% -> 0% of each run, Pallas kernels for 0% -> 10%
where the time goes in v1:
time: 63.1 us; the launch traced here: 62.8 us
  blocking collectives  37.6 us (60%)
  Pallas kernels  10.6 us (17%)
  starting transfers between devices  9.71 us (15%)
  waiting for transfers between devices  4.28 us (7%)
  between operations  0.67 us (1%)
    all_to_all x1, blocking collectives, body(): arrived = lax.all_to_all(own, 'wn', split_axis=0, concat_axis=0, tiled=True)  23.2 us
    all_to_all x1, blocking collectives, body(): back = lax.all_to_all(send, 'wn', split_axis=0, concat_axis=0, tiled=True)  14.4 us
    ppermute x1, starting transfers between devices, body(): second_in = lax.ppermute(second, ('wn', 'sw'), far)  7.79 us
    pallas_call x1, Pallas kernels, body(): call(inner_kernel, [fine, jax.ShapeDtypeStruct((5, 16, FINE), f32), jax.S...  5.17 us
    ppermute x1, waiting for transfers between devices, body(): second_in = lax.ppermute(second, ('wn', 'sw'), far)  4.27 us
    ppermute x1, starting transfers between devices, body(): first_in = lax.ppermute(first, ('wn', 'sw'), near)  1.92 us
    pallas_call x1, Pallas kernels, body(): call(far_kernel, [fine, jax.ShapeDtypeStruct((OWNERS, 4, 128), bf16)], [V...  1.85 us
  transfers between devices with their start and end apart: 2, of which 1 were waited for; matrix products, arithmetic and copies ran while one was open for 0% of the time, Pallas kernels for 10%

profile of v1, /device:TPU:30, one launch (start us, length us, event | category | flops | bytes accessed | tf_op | source)
XLA Modules:
  0.0 62.8 jit_solution(5935796724149113227)
XLA Ops:
  0.6 1.2 %shard_map.77 = (bf16[16,4,384]{2,1,0:T(4,128)(2,1)S(1)}, bf16[6,12,3072]{2,1,0:T(8,128)(2,1)S(1)}, s32[24,128]{1,0:T(8,128)S(1)}, f32[1,3072]{1,0:T(1,128)S(1)}...) custom-call(bf16[3,2,16,4,64]{4,3,2,1,0:T(4,128)(2,1)} %velocity_hbm.1, bf16[6,12,3072]{2,1,0:T(8,128)(2,1)} %salinity_hbm.1, ...), custom_call_target="tpu_custom_call" | custom-call | tf_op jit(solution)/shard_map/pallas_call | solution.py:389
  1.9 23.2 %all_to_all.10.arrived = bf16[16,4,384]{2,1,0:T(4,128)(2,1)S(1)} all-to-all(bf16[16,4,384]{2,1,0:T(4,128)(2,1)S(1)} %get-tuple-element.22), channel_id=1, replica_groups=mesh['wn'=16,'sw'=32] {'wn'}, dimensions={0} | all-to-all | bytes 98304 | tf_op jit(solution)/shard_map/all_to_all | solution.py:403
  25.0 0.4 shard_map.78
  25.5 7.8 %collective-permute-start = (bf16[24,1024]{1,0:T(8,128)(2,1)S(1)}, bf16[24,1024]{1,0:T(8,128)(2,1)S(1)}, u32[]{:S(2)}, u32[]{:S(2)}) collective-permute-start(bf16[24,1024]{1,0:T(8,128)(2,1)S(1)} %get-tuple-element.23), channel_id=1, source_target_pairs={{0,511},{1,2},{2,1},{3,4},{4,3},{5,6},{6,5},{7,8},{8,7},{9,10},{10... | collective-permute-start | bytes 147464 | tf_op jit(solution)/shard_map/ppermute | solution.py:407
  33.3 1.9 %collective-permute-start.1 = (bf16[24,1024]{1,0:T(8,128)(2,1)S(1)}, bf16[24,1024]{1,0:T(8,128)(2,1)S(1)}, u32[]{:S(2)}, u32[]{:S(2)}) collective-permute-start(bf16[24,1024]{1,0:T(8,128)(2,1)S(1)} %get-tuple-element.24), channel_id=1, source_target_pairs={{0,1},{1,0},{2,3},{3,2},{4,5},{5,4},{6,7},{7,6},{8,9},{9,8},{10,11... | collective-permute-start | bytes 147464 | tf_op jit(solution)/shard_map/ppermute | solution.py:408
  35.2 5.2 %shard_map.79 = (bf16[6,12,3072]{2,1,0:T(8,128)(2,1)S(1)}, f32[5,16,3072]{2,1,0:T(8,128)S(1)}, f32[8,3072]{1,0:T(8,128)S(1)}, bf16[24,256,128]{2,1,0:T(8,128)(2,1)S(1)}, bf16[24,128,256]{2,1,0:T(8,128)(2,1)S(1)}) custom-call(bf16[6,12,3072]{2,1,0:T(8,128)(2,1)S(1)} %get-tuple-element.21.salinity, f32[32,1024]{1,0:T(8,128)S(1)} %get-tuple-element.25.coarse, ...), custom_call_target="tpu_custom_call" | custom-call | flops 4000000000 | bytes 2000000000 | tf_op jit(solution)/shard_map/pallas_call | solution.py:409
  40.4 0.0 collective-permute-done.1.message
  40.4 1.2 %shard_map.80 = (bf16[6,12,3072]{2,1,0:T(8,128)(2,1)S(1)}, f32[8,3072]{1,0:T(8,128)S(1)}, f32[16,1024]{1,0:T(8,128)S(1)}) custom-call(bf16[24,1024]{1,0:T(8,128)(2,1)S(1)} %collective-permute-done.1.message, bf16[6,12,3072]{2,1,0:T(8,128)(2,1)S(1)} %get-tuple-element.30.inner, f32[5,16,3072]{2,1,0:T(8,128)S(1)} %get-tuple-element.31.edges, ...), custom_call_target="tpu_custom_call" | custom-call | flops 1000 | bytes 1000 | tf_op jit(solution)/shard_map/pallas_call | solution.py:435
  41.6 4.3 %collective-permute-done.message = bf16[24,1024]{1,0:T(8,128)(2,1)S(1)} collective-permute-done((bf16[24,1024]{1,0:T(8,128)(2,1)S(1)}, bf16[24,1024]{1,0:T(8,128)(2,1)S(1)}, u32[]{:S(2)}, u32[]{:S(2)}) %collective-permute-start) | collective-permute-done | bytes 49184 | tf_op jit(solution)/shard_map/ppermute | solution.py:407
  45.9 1.8 %shard_map.81 = (bf16[6,12,3072]{2,1,0:T(8,128)(2,1)}, bf16[16,4,128]{2,1,0:T(4,128)(2,1)S(1)}) custom-call(bf16[24,1024]{1,0:T(8,128)(2,1)S(1)} %collective-permute-done.message, bf16[6,12,3072]{2,1,0:T(8,128)(2,1)S(1)} %get-tuple-element.35.near, f32[8,3072]{1,0:T(8,128)S(1)} %get-tuple-element.36.sums, f32[16,1024]{1,0:T(8,128)S(1)} %get-tuple-element.37.near_total, ...), custom_call_target="tpu_custom_call" | custom-call | tf_op jit(solution)/shard_map/pallas_call | solution.py:442
  47.7 14.4 %all_to_all.11.arrived = bf16[16,4,128]{2,1,0:T(4,128)(2,1)S(1)} all-to-all(bf16[16,4,128]{2,1,0:T(4,128)(2,1)S(1)} %get-tuple-element.39), channel_id=1, replica_groups=mesh['wn'=16,'sw'=32] {'wn'}, dimensions={0} | all-to-all | bytes 32768 | tf_op jit(solution)/shard_map/all_to_all | solution.py:456
  62.1 0.7 %shard_map.82 = bf16[2,16,4,64]{3,2,1,0:T(4,128)(2,1)} custom-call(bf16[16,4,128]{2,1,0:T(4,128)(2,1)S(1)} %all_to_all.11.arrived), custom_call_target="tpu_custom_call" | custom-call | tf_op jit(solution)/shard_map/pallas_call | solution.py:457
Async XLA Ops:
  25.5 20.4 %collective-permute-start = (bf16[24,1024]{1,0:T(8,128)(2,1)S(1)}, bf16[24,1024]{1,0:T(8,128)(2,1)S(1)}, u32[]{:S(2)}, u32[]{:S(2)}) collective-permute-start(bf16[24,1024]{1,0:T(8,128)(2,1)S(1)} %get-tuple-element.23), channel_id=1, source_target_pairs={{0,511},{1,2},{2,1},{3,4},{4,3},{5,6},{6,5},{7,8},{8,7},{9,10},{10... | collective-permute-start | bytes 147464 | tf_op jit(solution)/shard_map/ppermute | solution.py:407
  33.3 7.1 %collective-permute-start.1 = (bf16[24,1024]{1,0:T(8,128)(2,1)S(1)}, bf16[24,1024]{1,0:T(8,128)(2,1)S(1)}, u32[]{:S(2)}, u32[]{:S(2)}) collective-permute-start(bf16[24,1024]{1,0:T(8,128)(2,1)S(1)} %get-tuple-element.24), channel_id=1, source_target_pairs={{0,1},{1,0},{2,3},{3,2},{4,5},{5,4},{6,7},{7,6},{8,9},{9,8},{10,11... | collective-permute-start | bytes 147464 | tf_op jit(solution)/shard_map/ppermute | solution.py:408

commit v2 on v1

--- a/solution.py
+++ b/solution.py
@@ -18,6 +18,8 @@
 SLAB = 64
 BLOCK = 128
 BLOCKS = FINE // BLOCK
+ORDER = [6, 7, 8, 9, 10, 11, 12, 13, 14, 15, 0, 1, 2, 3, 4, 5]
+SLOT = [ORDER.index(q) for q in range(16)]
 WINDOW = 256
 STACK = 32
 HALO_ROWS = 24
@@ -114,7 +116,7 @@
     for q in range(OWNERS):
         for c in range(3):
             for p in range(2):
-                send[q, :, c * 128 + p * 64 : c * 128 + p * 64 + 64] = velocity[c, p, q]
+                send[SLOT[q], :, c * 128 + p * 64 : c * 128 + p * 64 + 64] = velocity[c, p, q]
     for copy in copies[1:]:
         copy.wait()
 
@@ -125,8 +127,8 @@
     for t in range(8):
         lanes = slice(t * 128, t * 128 + 128)
         for c in range(3):
-            one = arrived[2 * t, :, c * 128 : c * 128 + 128].astype(f32)
-            two = arrived[2 * t + 1, :, c * 128 : c * 128 + 128].astype(f32)
+            one = arrived[SLOT[2 * t], :, c * 128 : c * 128 + 128].astype(f32)
+            two = arrived[SLOT[2 * t + 1], :, c * 128 : c * 128 + 128].astype(f32)
             coarse[c * 4 : c * 4 + 4, lanes] = jnp.where(left, one, pltpu.roll(two, 64, 1))
             coarse[16 + c * 4 : 20 + c * 4, lanes] = jnp.where(left, pltpu.roll(one, 64, 1), two)
     coarse[12:16, :] = jnp.zeros((4, COARSE), f32)
@@ -235,6 +237,7 @@
         raw[:, lanes] = jnp.dot(sources[:, pl.ds(starts[b], WINDOW)], hits[b], preferred_element_type=f32)
     results = []
     spare = jnp.zeros((2, CHUNK), f32)
+    planes = lax.broadcasted_iota(jnp.int32, (8, CHUNK), 0)
     for k in range(FINE // CHUNK):
         lanes = slice(k * CHUNK, k * CHUNK + CHUNK)
         weight = wall_weight[:, lanes]
@@ -250,7 +253,7 @@
         new = edges[0, at, lanes] + FLAT * ghost + edges[1, at, lanes] * pull
         new = new + velocity[0:8] * (pull - edges[2, at, lanes])
         new = new - velocity[8:16] * edges[3, at, lanes] - velocity[16:24] * edges[4, at, lanes]
-        results.append(new.astype(bf16))
+        results.append(jnp.where(planes < PLANES, new, 0.0).astype(bf16))
     return results
 
 
@@ -347,8 +350,8 @@
     for t in range(8):
         tile = restricted[:, t * 128 : t * 128 + 128]
         turned = pltpu.roll(tile, 64, 1)
-        send[2 * t] = jnp.where(left, tile[0:4], turned[4:8]).astype(bf16)
-        send[2 * t + 1] = jnp.where(left, turned[0:4], tile[4:8]).astype(bf16)
+        send[SLOT[2 * t]] = jnp.where(left, tile[0:4], turned[4:8]).astype(bf16)
+        send[SLOT[2 * t + 1]] = jnp.where(left, turned[0:4], tile[4:8]).astype(bf16)
     for copy in copies:
         copy.wait()
 
@@ -356,7 +359,7 @@
 def spread_kernel(arrived, coarse):
     for q in range(OWNERS):
         for p in range(2):
-            coarse[p, q] = arrived[q, :, p * 64 : p * 64 + 64]
+            coarse[p, q] = arrived[SLOT[q], :, p * 64 : p * 64 + 64]
 
 
 VMEM = pl.BlockSpec(memory_space=pltpu.VMEM)
@@ -400,7 +403,7 @@
         [pltpu.VMEM((3, 2, OWNERS, 4, SLAB), bf16), pltpu.SemaphoreType.DMA((6,))],
         megabytes=56,
     )(velocity, salinity, wall_index.reshape(BLOCKS, BLOCK), wall_weight[None], spacing[None], matrices)
-    arrived = lax.all_to_all(own, "wn", split_axis=0, concat_axis=0, tiled=True)
+    arrived = lax.all_to_all(own, "wn", split_axis=0, concat_axis=0, tiled=True, axis_index_groups=[ORDER])
     second, first, coarse = call(
         edge_kernel, [message, message, jax.ShapeDtypeStruct((STACK, COARSE), f32)], [VMEM] * 2
     )(salinity, arrived)
@@ -453,7 +456,7 @@
         ],
         out_specs=[ANY, VMEM],
     )(second_in, near_updated, sums, near_total, edges, hits, turned_hits, wall_index, wall_weight, matrices)
-    back = lax.all_to_all(send, "wn", split_axis=0, concat_axis=0, tiled=True)
+    back = lax.all_to_all(send, "wn", split_axis=0, concat_axis=0, tiled=True, axis_index_groups=[ORDER])
     coarse = call(spread_kernel, jax.ShapeDtypeStruct((2, OWNERS, 4, SLAB), bf16), [VMEM])(back)
     return (updated, coarse)
 

time: 63.1 us -> 60.5 us (0.959)
  blocking collectives: 37.6 us -> 32.6 us
  waiting for transfers between devices: 4.28 us -> 6.64 us
    all_to_all x2, blocking collectives: 37.6 us -> 32.6 us  [the longest x1 20.5 us: body(): lax.all_to_all(own, 'wn', split_axis=0, concat_axis=0, tiled=True, axis_i...]
    ppermute x1, waiting for transfers between devices: 4.27 us -> 6.64 us  [body(): second_in = lax.ppermute(second, ('wn', 'sw'), far)]
  transfers between devices with their start and end apart: 2 -> 2, of which waited for: 1 -> 1; matrix products, arithmetic and copies ran while one was open for 0% -> 0% of each run, Pallas kernels for 10% -> 11%
where the time goes in v2:
time: 60.5 us; the launch traced here: 60.3 us
  blocking collectives  32.6 us (54%)
  Pallas kernels  10.6 us (18%)
  starting transfers between devices  9.71 us (16%)
  waiting for transfers between devices  6.64 us (11%)
  between operations  0.68 us (1%)
    all_to_all x1, blocking collectives, body(): lax.all_to_all(own, 'wn', split_axis=0, concat_axis=0, tiled=True, axis_i...  20.5 us
    all_to_all x1, blocking collectives, body(): lax.all_to_all(send, 'wn', split_axis=0, concat_axis=0, tiled=True, axis_...  12.2 us
    ppermute x1, starting transfers between devices, body(): second_in = lax.ppermute(second, ('wn', 'sw'), far)  7.79 us
    ppermute x1, waiting for transfers between devices, body(): second_in = lax.ppermute(second, ('wn', 'sw'), far)  6.64 us
    pallas_call x1, Pallas kernels, body(): call(inner_kernel, [fine, jax.ShapeDtypeStruct((5, 16, FINE), f32), jax.S...  5.17 us
    ppermute x1, starting transfers between devices, body(): first_in = lax.ppermute(first, ('wn', 'sw'), near)  1.92 us
    pallas_call x1, Pallas kernels, body(): call(far_kernel, [fine, jax.ShapeDtypeStruct((OWNERS, 4, 128), bf16)], [V...  1.84 us
    pallas_call x1, Pallas kernels, body(): call(near_kernel, [fine, jax.ShapeDtypeStruct((8, FINE), f32), jax.ShapeD...  1.23 us
  transfers between devices with their start and end apart: 2, of which 1 were waited for; matrix products, arithmetic and copies ran while one was open for 0% of the time, Pallas kernels for 11%

profile of v2, /device:TPU:30, one launch (start us, length us, event | category | flops | bytes accessed | tf_op | source)
XLA Modules:
  0.0 60.3 jit_solution(12610917490688714101)
XLA Ops:
  0.6 1.2 %shard_map.77 = (bf16[16,4,384]{2,1,0:T(4,128)(2,1)S(1)}, bf16[6,12,3072]{2,1,0:T(8,128)(2,1)S(1)}, s32[24,128]{1,0:T(8,128)S(1)}, f32[1,3072]{1,0:T(1,128)S(1)}...) custom-call(bf16[3,2,16,4,64]{4,3,2,1,0:T(4,128)(2,1)} %velocity_hbm.1, bf16[6,12,3072]{2,1,0:T(8,128)(2,1)} %salinity_hbm.1, ...), custom_call_target="tpu_custom_call" | custom-call | tf_op jit(solution)/shard_map/pallas_call | solution.py:392
  1.9 20.5 %all_to_all.10.arrived = bf16[16,4,384]{2,1,0:T(4,128)(2,1)S(1)} all-to-all(bf16[16,4,384]{2,1,0:T(4,128)(2,1)S(1)} %get-tuple-element.22), channel_id=1, replica_groups={{192,224,256,288,320,352,384,416,448,480,0,32,64,96,128,160},{193,225,2..., dimensions={0} | all-to-all | bytes 98304 | tf_op jit(solution)/shard_map/all_to_all | solution.py:406
  22.3 0.4 shard_map.78
  22.8 7.8 %collective-permute-start = (bf16[24,1024]{1,0:T(8,128)(2,1)S(1)}, bf16[24,1024]{1,0:T(8,128)(2,1)S(1)}, u32[]{:S(2)}, u32[]{:S(2)}) collective-permute-start(bf16[24,1024]{1,0:T(8,128)(2,1)S(1)} %get-tuple-element.23), channel_id=1, source_target_pairs={{0,511},{1,2},{2,1},{3,4},{4,3},{5,6},{6,5},{7,8},{8,7},{9,10},{10... | collective-permute-start | bytes 147464 | tf_op jit(solution)/shard_map/ppermute | solution.py:410
  30.6 1.9 %collective-permute-start.1 = (bf16[24,1024]{1,0:T(8,128)(2,1)S(1)}, bf16[24,1024]{1,0:T(8,128)(2,1)S(1)}, u32[]{:S(2)}, u32[]{:S(2)}) collective-permute-start(bf16[24,1024]{1,0:T(8,128)(2,1)S(1)} %get-tuple-element.24), channel_id=1, source_target_pairs={{0,1},{1,0},{2,3},{3,2},{4,5},{5,4},{6,7},{7,6},{8,9},{9,8},{10,11... | collective-permute-start | bytes 147464 | tf_op jit(solution)/shard_map/ppermute | solution.py:411
  32.5 5.2 %shard_map.79 = (bf16[6,12,3072]{2,1,0:T(8,128)(2,1)S(1)}, f32[5,16,3072]{2,1,0:T(8,128)S(1)}, f32[8,3072]{1,0:T(8,128)S(1)}, bf16[24,256,128]{2,1,0:T(8,128)(2,1)S(1)}, bf16[24,128,256]{2,1,0:T(8,128)(2,1)S(1)}) custom-call(bf16[6,12,3072]{2,1,0:T(8,128)(2,1)S(1)} %get-tuple-element.21.salinity, f32[32,1024]{1,0:T(8,128)S(1)} %get-tuple-element.25.coarse, ...), custom_call_target="tpu_custom_call" | custom-call | flops 4000000000 | bytes 2000000000 | tf_op jit(solution)/shard_map/pallas_call | solution.py:412
  37.7 0.0 collective-permute-done.1.message
  37.7 1.2 %shard_map.80 = (bf16[6,12,3072]{2,1,0:T(8,128)(2,1)S(1)}, f32[8,3072]{1,0:T(8,128)S(1)}, f32[16,1024]{1,0:T(8,128)S(1)}) custom-call(bf16[24,1024]{1,0:T(8,128)(2,1)S(1)} %collective-permute-done.1.message, bf16[6,12,3072]{2,1,0:T(8,128)(2,1)S(1)} %get-tuple-element.30.inner, f32[5,16,3072]{2,1,0:T(8,128)S(1)} %get-tuple-element.31.edges, ...), custom_call_target="tpu_custom_call" | custom-call | flops 1000 | bytes 1000 | tf_op jit(solution)/shard_map/pallas_call | solution.py:438
  38.9 6.6 %collective-permute-done.message = bf16[24,1024]{1,0:T(8,128)(2,1)S(1)} collective-permute-done((bf16[24,1024]{1,0:T(8,128)(2,1)S(1)}, bf16[24,1024]{1,0:T(8,128)(2,1)S(1)}, u32[]{:S(2)}, u32[]{:S(2)}) %collective-permute-start) | collective-permute-done | bytes 49184 | tf_op jit(solution)/shard_map/ppermute | solution.py:410
  45.6 1.8 %shard_map.81 = (bf16[6,12,3072]{2,1,0:T(8,128)(2,1)}, bf16[16,4,128]{2,1,0:T(4,128)(2,1)S(1)}) custom-call(bf16[24,1024]{1,0:T(8,128)(2,1)S(1)} %collective-permute-done.message, bf16[6,12,3072]{2,1,0:T(8,128)(2,1)S(1)} %get-tuple-element.35.near, f32[8,3072]{1,0:T(8,128)S(1)} %get-tuple-element.36.sums, f32[16,1024]{1,0:T(8,128)S(1)} %get-tuple-element.37.near_total, ...), custom_call_target="tpu_custom_call" | custom-call | tf_op jit(solution)/shard_map/pallas_call | solution.py:445
  47.4 12.2 %all_to_all.11.arrived = bf16[16,4,128]{2,1,0:T(4,128)(2,1)S(1)} all-to-all(bf16[16,4,128]{2,1,0:T(4,128)(2,1)S(1)} %get-tuple-element.39), channel_id=1, replica_groups={{192,224,256,288,320,352,384,416,448,480,0,32,64,96,128,160},{193,225,2..., dimensions={0} | all-to-all | bytes 32768 | tf_op jit(solution)/shard_map/all_to_all | solution.py:459
  59.6 0.7 %shard_map.82 = bf16[2,16,4,64]{3,2,1,0:T(4,128)(2,1)} custom-call(bf16[16,4,128]{2,1,0:T(4,128)(2,1)S(1)} %all_to_all.11.arrived), custom_call_target="tpu_custom_call" | custom-call | tf_op jit(solution)/shard_map/pallas_call | solution.py:460
Async XLA Ops:
  22.8 22.8 %collective-permute-start = (bf16[24,1024]{1,0:T(8,128)(2,1)S(1)}, bf16[24,1024]{1,0:T(8,128)(2,1)S(1)}, u32[]{:S(2)}, u32[]{:S(2)}) collective-permute-start(bf16[24,1024]{1,0:T(8,128)(2,1)S(1)} %get-tuple-element.23), channel_id=1, source_target_pairs={{0,511},{1,2},{2,1},{3,4},{4,3},{5,6},{6,5},{7,8},{8,7},{9,10},{10... | collective-permute-start | bytes 147464 | tf_op jit(solution)/shard_map/ppermute | solution.py:410
  30.6 7.1 %collective-permute-start.1 = (bf16[24,1024]{1,0:T(8,128)(2,1)S(1)}, bf16[24,1024]{1,0:T(8,128)(2,1)S(1)}, u32[]{:S(2)}, u32[]{:S(2)}) collective-permute-start(bf16[24,1024]{1,0:T(8,128)(2,1)S(1)} %get-tuple-element.24), channel_id=1, source_target_pairs={{0,1},{1,0},{2,3},{3,2},{4,5},{5,4},{6,7},{7,6},{8,9},{9,8},{10,11... | collective-permute-start | bytes 147464 | tf_op jit(solution)/shard_map/ppermute | solution.py:411
